TPU v7x, 32 devices: a whole 2x2x4 slice. The times are simulated.
32 devices in a mesh: gx: 4 (over z), gy: 2 (over y), gz: 4 (over x, core).
Axes of the slice: x: 2, y: 2, z: 4, core: 2. Of those that a mesh axis runs over, the one named last changes fastest.
Arguments:
- orbitals: float32 [2, 64, 32, 512], P(None, 'gx', 'gy', 'gz'), may hold values from -6 to 6
- potential: float32 [64, 32, 512], P('gx', 'gy', 'gz'), may hold values from -2 to 1
- projectors: float32 [4, 2, 4, 8, 4, 4, 4096], P('gx', 'gy', 'gz'), as said below
- coupling: float32 [4, 2, 4, 8, 4, 4, 4], P('gx', 'gy', 'gz'), as said below
- block_starts: int32 [4, 2, 4, 8, 4, 3], P('gx', 'gy', 'gz'), may hold values from 0 to 127, as said below
- owner_counts: int32 [4, 2, 4, 8], P('gx', 'gy', 'gz'), may hold values from 1 to 4, as said below
Outputs:
- applied: float32 [2, 64, 32, 512], P(None, 'gx', 'gy', 'gz')
Inputs may be any that keep to these rules, and one draw needn't show every extreme that they name: `block_starts`: entry [q, o, s, d] is the start along dimension d, inside its owner box, of the block of slot s of the box q - o (periodically, o = (a, b, c) with c fastest); it is below 16, 16, 128 for d = 0, 1, 2, and all eight copies of an atom agree. `owner_counts`: entry [q, o] is the number of live slots of the box q - o (periodically, o ordered as in block_starts); the eight copies agree. `projectors`: the eight copies of an atom's values agree. `coupling`: the eight copies of an atom's matrix agree.
All inputs are finite; a program needn't handle non-finite values.
Results may differ from a plain program's by a relative error of at most 0.00005.
Values sent between devices are 32-bit elements; how exact they have to be, the bound alone decides.
A program may use at most 64 MiB of HBM per device.

v0:
```python
import functools

import jax
import jax.numpy as jnp
from jax import lax
from jax.experimental import pallas as pl
from jax.experimental.pallas import tpu as pltpu
from jax.sharding import PartitionSpec as P

MESH = pl.DeviceIdType.MESH
HI = lax.Precision.HIGHEST
F32 = jnp.float32
COEFF = [
    -5369.0 / 1800.0,
    12.0 / 7.0,
    -15.0 / 56.0,
    10.0 / 189.0,
    -1.0 / 112.0,
    2.0 / 1925.0,
    -1.0 / 16632.0,
]
PAD = 40


def iota(shape, dim):
    return lax.broadcasted_iota(jnp.int32, shape, dim)


def band(distance):
    d = jnp.abs(distance)
    out = jnp.zeros(distance.shape, F32)
    for k in range(1, 7):
        out = jnp.where(d == k, -0.5 * COEFF[k], out)
    return out


def shear(v, back):
    axis = v.ndim - 1
    sub = iota(v.shape, axis - 1)
    for bit in (1, 2, 4):
        turn = (128 - 16 * bit) if back else 16 * bit
        v = jnp.where((sub & bit) != 0, pltpu.roll(v, turn, axis), v)
    return v


def residues(n):
    return [0, 1] if n == 2 else [0, 1, n - 1]


def kernel(
    sizes,
    x_hbm, pot_hbm, p_hbm, cpl_ref, st_ref, cnt_ref,
    out_ref,
    xpad, xe, ye, pot, pv, pr, sheared, accs, zs, zr, recv, zc, wrep, cs, mprime,
    lsem, hsend, hrecv, psend, precv,
):
    names = ("gx", "gy", "gz")
    me = [lax.axis_index(name) for name in names]
    res = [residues(n) for n in sizes]
    slots = {}
    for ex in res[0]:
        for ey in res[1]:
            for ez in res[2]:
                slots[(ex, ey, ez)] = len(slots)

    def device(offset):
        return tuple(lax.rem(me[d] + offset[d] % sizes[d], sizes[d]) for d in range(3))

    def slot_of(offset):
        return slots[tuple(offset[d] % sizes[d] for d in range(3))]

    load_x = pltpu.make_async_copy(x_hbm, xe.at[:, 6:22], lsem.at[0])
    load_y = pltpu.make_async_copy(x_hbm, ye.at[:, :, 8:24], lsem.at[1])
    load_p = pltpu.make_async_copy(p_hbm, pv, lsem.at[2])
    load_pot = pltpu.make_async_copy(pot_hbm, pot, lsem.at[3])
    load_x.start()
    load_p.start()
    load_y.start()
    load_pot.start()

    barrier = pltpu.get_barrier_semaphore()
    others = [e for e in slots if e != (0, 0, 0)]
    for e in others:
        pl.semaphore_signal(barrier, inc=1, device_id=device(e), device_id_type=MESH)

    def clear(i, carry):
        for b in range(2):
            xpad[b, i] = jnp.zeros((48, 128), F32)
        return carry

    lax.fori_loop(0, 48, clear, 0)
    for b in range(2):
        zc[b] = jnp.zeros((112, 128), F32)

    for s in range(4):
        for i in range(4):
            cs[pl.ds((s * 4 + i) * 4, 4), :] = cpl_ref[s, i]
    pick = (iota((256, 8), 0) // 32 == iota((256, 8), 1)).astype(F32)
    per_row = lax.dot_general(pick, cs[...], (((1,), (1,)), ((), ())), precision=HI,
                              preferred_element_type=F32)
    r64, c64 = iota((256, 64), 0), iota((256, 64), 1)
    own = ((r64 // 8) % 4 == c64 // 16) & (r64 % 4 == (c64 // 4) % 4)
    per_row = jnp.where(own, per_row, 0.0)
    spread = (iota((64, 256), 0) % 4 == iota((64, 256), 1) % 4).astype(F32)
    wide = lax.dot_general(per_row, spread, (((1,), (0,)), ((), ())), precision=HI,
                           preferred_element_type=F32)
    same = iota((256, 256), 0) // 4 == iota((256, 256), 1) // 4
    mprime[...] = jnp.where(same, wide, 0.0)

    pl.semaphore_wait(barrier, len(others))

    sends = []

    def send(src, dst, k, offset):
        copy = pltpu.make_async_remote_copy(
            src_ref=src, dst_ref=dst, send_sem=hsend.at[k], recv_sem=hrecv.at[k],
            device_id=device(offset), device_id_type=MESH,
        )
        copy.start()
        sends.append(copy)

    send(x_hbm.at[:, :, 8:16, :], ye.at[:, :, 0:8, :], 0, (0, 1, 0))
    send(x_hbm.at[:, :, 0:8, :], ye.at[:, :, 24:32, :], 1, (0, -1, 0))
    send(x_hbm.at[:, 10:16], xe.at[:, 0:6], 2, (1, 0, 0))
    send(x_hbm.at[:, 0:6], xe.at[:, 22:28], 3, (-1, 0, 0))

    load_x.wait()

    def lay(x, carry):
        for b in range(2):
            xpad[b, 16 + x, 16:32, :] = shear(xe[b, 6 + x], False)
            sheared[b, x] = jnp.zeros((16, 128), F32)
        return carry

    lax.fori_loop(0, 16, lay, 0)
    flat = xe[:, 6:22].reshape(512, 128)
    row, col = iota((16, 128), 0), iota((16, 128), 1)
    sel = (col == jnp.where(row < 8, 120 + row, row - 8)).astype(F32)
    zs[...] = lax.dot_general(sel, flat, (((1,), (1,)), ((), ())), precision=HI,
                              preferred_element_type=F32)
    send(zs.at[0:8], zr.at[0:8], 4, (0, 0, 1))
    send(zs.at[8:16], zr.at[8:16], 5, (0, 0, -1))
    load_p.wait()

    lane, sub = iota((8, 128), 1), iota((8, 128), 0)

    def place(n):
        o, s = n >> 2, n & 3
        a = st_ref[0, s, o] - 16 * (o >> 2)
        b0 = st_ref[1, s, o] - 16 * ((o >> 1) & 1)
        c = st_ref[2, s, o] - 128 * (o & 1)
        return o, s, a, b0, c

    def turn(n, carry):
        _, _, _, b0, c = place(n)
        by = (c + 16 * b0) & 127
        for i in range(4):
            plane = pv[pl.ds(n * 128 + i, 32, stride=4), :]
            pr[pl.ds(n * 128 + i * 32, 32), :] = pltpu.roll(plane, by, 1)
        return carry

    lax.fori_loop(0, 32, turn, 0)

    def gather(n, carry):
        _, _, a, b0, c = place(n)
        z = (lane - 16 * (sub + b0)) & 127
        keep = (z >= c) & (z < c + 16)
        acc = [jnp.zeros((8, 128), F32) for _ in range(8)]
        for x in range(16):
            for yh in range(2):
                rows = [
                    jnp.broadcast_to(pr[pl.ds(n * 128 + i * 32 + x * 2 + yh, 1), :], (8, 128))
                    for i in range(4)
                ]
                for b in range(2):
                    g = xpad[b, 16 + a + x, pl.ds(16 + b0 + 8 * yh, 8), :]
                    g = jnp.where(keep, g, 0.0)
                    for i in range(4):
                        acc[b * 4 + i] = acc[b * 4 + i] + g * rows[i]
        for k in range(8):
            accs[pl.ds(n * 64 + k * 8, 8), :] = acc[k]
        return carry

    lax.fori_loop(0, 32, gather, 0)

    total = accs[pl.ds(0, 256, stride=8), :]
    for k in range(1, 8):
        total = total + accs[pl.ds(k, 256, stride=8), :]
    mine = lax.dot_general(jnp.ones((8, 128), F32), total, (((1,), (1,)), ((), ())),
                           precision=HI, preferred_element_type=F32)
    recv[0] = mine[0:1]
    parts = []
    for k, e in enumerate(others):
        copy = pltpu.make_async_remote_copy(
            src_ref=recv.at[0], dst_ref=recv.at[slot_of(tuple(-v for v in e))],
            send_sem=psend.at[k], recv_sem=precv.at[slot_of(tuple(-v for v in e))],
            device_id=device(e), device_id_type=MESH,
        )
        copy.start()
        parts.append(copy)

    load_y.wait()
    load_pot.wait()
    r128, c128 = iota((128, 128), 0), iota((128, 128), 1)
    near = jnp.where(r128 == c128, -0.5 * 3.0 * COEFF[0], band(r128 - c128))
    out_ref[...] = lax.dot_general(flat, near, (((1,), (0,)), ((), ())), precision=HI,
                                   preferred_element_type=F32).reshape(2, 16, 16, 128)
    for copy in sends:
        copy.wait()
    far = band(jnp.where(row < 8, row - 8, 120 + row) - col)
    edge = lax.dot_general(zr[...], far, (((0,), (0,)), ((), ())), precision=HI,
                           preferred_element_type=F32).reshape(2, 16, 16, 128)
    out_ref[...] += edge

    def stencil(x, carry):
        for b in range(2):
            acc = pot[x] * xe[b, x + 6] + out_ref[b, x]
            for k in range(1, 7):
                four = (ye[b, x, 8 - k : 24 - k, :] + ye[b, x, 8 + k : 24 + k, :]) + (
                    xe[b, x + 6 - k] + xe[b, x + 6 + k]
                )
                acc = acc + (-0.5 * COEFF[k]) * four
            out_ref[b, x] = acc
        return carry

    lax.fori_loop(0, 16, stencil, 0)

    for copy in parts:
        copy.wait()

    def got(dx, dy, dz):
        r = recv[slot_of((dx, dy, dz))]
        return r[:, 0:128], r[:, 128:256]

    lane1 = iota((1, 128), 1)
    upper_y, upper_z = (lane1 & 64) != 0, (lane1 & 32) != 0
    halves = []
    for h in range(2):
        by_z = {}
        for dz in (-1, 0, 1):
            by_y = {}
            for dy in (-1, 0, 1):
                by_y[dy] = got(0, dy, dz)[h] + got(1 - 2 * h, dy, dz)[1 - h]
            crossed = jnp.where(upper_y, by_y[1], by_y[-1])
            by_z[dz] = by_y[0] + pltpu.roll(crossed, 64, 1)
        down = pltpu.roll(by_z[1], 96, 1)
        up = pltpu.roll(by_z[-1], 32, 1)
        halves.append(by_z[0] + jnp.where(upper_z, up, down))
    sums = jnp.concatenate(halves, axis=1)
    wrep[...] = lax.dot_general(mprime[...] * sums, jnp.ones((256, 128), F32),
                                (((1,), (0,)), ((), ())), precision=HI,
                                preferred_element_type=F32)

    def scatter(n, carry):
        o, s, a, b0, c = place(n)
        live = jnp.where(s < cnt_ref[o], 1.0, 0.0).astype(F32)
        planes = [pr[pl.ds(n * 128 + i * 32, 32), :] for i in range(4)]
        for b in range(2):
            mix = jnp.zeros((32, 128), F32)
            for i in range(4):
                mix = mix + planes[i] * (wrep[pl.ds(n * 8 + b * 4 + i, 1), :] * live)
            zc[b, PAD : PAD + 32, :] = mix
        low = b0 >> 3
        rest = b0 & 7
        first = sub >= rest
        z = (lane - 16 * sub) & 127
        window = (z >= c) & (z < c + 16)
        for t in range(2):
            y = 8 * t + sub - b0
            keep = window & (y >= 0) & (y < 16)
            start = PAD - 2 * a + t - low
            for x in range(16):
                for b in range(2):
                    one = jnp.broadcast_to(zc[b, pl.ds(start + 2 * x, 1), :], (8, 128))
                    two = jnp.broadcast_to(zc[b, pl.ds(start + 2 * x - 1, 1), :], (8, 128))
                    v = jnp.where(first, one, two)
                    sheared[b, x, 8 * t : 8 * t + 8, :] += jnp.where(keep, v, 0.0)
        return carry

    lax.fori_loop(0, 32, scatter, 0)

    def finish(x, carry):
        for b in range(2):
            out_ref[b, x] += shear(sheared[b, x], True)
        return carry

    lax.fori_loop(0, 16, finish, 0)


def solution(mesh):
    sizes = tuple(mesh.shape[name] for name in ("gx", "gy", "gz"))
    nslots = 1
    for n in sizes:
        nslots *= len(residues(n))

    def on_device(orbitals, potential, projectors, coupling, block_starts, owner_counts):
        rows = projectors.reshape(32, 4, 32, 128).transpose(0, 2, 1, 3).reshape(4096, 128)
        matrices = coupling.reshape(8, 4, 4, 4).transpose(1, 2, 3, 0)
        starts = block_starts.reshape(8, 4, 3).transpose(2, 1, 0)
        counts = owner_counts.reshape(8)
        anyspace = pl.BlockSpec(memory_space=pl.ANY)
        vmem = pl.BlockSpec(memory_space=pltpu.VMEM)
        smem = pl.BlockSpec(memory_space=pltpu.SMEM)
        return pl.pallas_call(
            functools.partial(kernel, sizes),
            out_shape=jax.ShapeDtypeStruct((2, 16, 16, 128), F32),
            in_specs=[anyspace, anyspace, anyspace, vmem, smem, smem],
            out_specs=vmem,
            scratch_shapes=[
                pltpu.VMEM((2, 48, 48, 128), F32),
                pltpu.VMEM((2, 28, 16, 128), F32),
                pltpu.VMEM((2, 16, 32, 128), F32),
                pltpu.VMEM((16, 16, 128), F32),
                pltpu.VMEM((4096, 128), F32),
                pltpu.VMEM((4096, 128), F32),
                pltpu.VMEM((2, 16, 16, 128), F32),
                pltpu.VMEM((2048, 128), F32),
                pltpu.VMEM((16, 512), F32),
                pltpu.VMEM((16, 512), F32),
                pltpu.VMEM((nslots, 1, 256), F32),
                pltpu.VMEM((2, 112, 128), F32),
                pltpu.VMEM((256, 128), F32),
                pltpu.VMEM((64, 8), F32),
                pltpu.VMEM((256, 256), F32),
                pltpu.SemaphoreType.DMA((4,)),
                pltpu.SemaphoreType.DMA((6,)),
                pltpu.SemaphoreType.DMA((6,)),
                pltpu.SemaphoreType.DMA((nslots,)),
                pltpu.SemaphoreType.DMA((nslots,)),
            ],
            compiler_params=pltpu.CompilerParams(
                collective_id=0, has_side_effects=True, vmem_limit_bytes=32 * 1024 * 1024
            ),
        )(orbitals, potential, rows, matrices, starts, counts)

    in_specs = (
        P(None, "gx", "gy", "gz"),
        P("gx", "gy", "gz"),
        P("gx", "gy", "gz", None, None, None, None),
        P("gx", "gy", "gz", None, None, None, None),
        P("gx", "gy", "gz", None, None, None),
        P("gx", "gy", "gz", None),
    )
    return jax.shard_map(
        on_device, mesh=mesh, in_specs=in_specs,
        out_specs=P(None, "gx", "gy", "gz"), check_vma=False,
    )
```

profile of v0, /device:TPU:0, one launch (start us, length us, event | category | flops | bytes accessed | tf_op | source)
XLA Modules:
  0.0 33.5 jit_solution(14877984928680492996)
XLA Ops:
  0.0 0.0 copy-start
  0.0 1.6 %copy-done = f32[1,1,1,8,4,4,4096]{6,5,4,3,2,1,0:T(4,128)S(1)} copy-done((f32[1,1,1,8,4,4,4096]{6,5,4,3,2,1,0:T(4,128)S(1)}, f32[1,1,1,8,4,4,4096]{6,5,4,3,2,1,0:T(4,128)}, u32[]{:S(2)}) %copy-start) | copy-done | bytes 2097176
  1.6 0.0 copy-start.1
  1.6 0.9 %copy-done.1 = f32[2,16,16,128]{3,2,1,0:T(8,128)S(1)} copy-done((f32[2,16,16,128]{3,2,1,0:T(8,128)S(1)}, f32[2,16,16,128]{3,2,1,0:T(8,128)}, u32[]{:S(2)}) %copy-start.1) | copy-done | bytes 262168
  2.5 0.0 copy-start.2
  2.5 0.9 %copy-done.2 = f32[16,16,128]{2,1,0:T(8,128)S(1)} copy-done((f32[16,16,128]{2,1,0:T(8,128)S(1)}, f32[16,16,128]{2,1,0:T(8,128)}, u32[]{:S(2)}) %copy-start.2) | copy-done | bytes 131096
  3.4 0.0 copy-start.3
  3.4 0.8 %copy-done.3 = f32[1,1,1,8,4,4,4]{3,6,5,4,2,1,0:T(4,128)S(1)} copy-done((f32[1,1,1,8,4,4,4]{3,6,5,4,2,1,0:T(4,128)S(1)}, f32[1,1,1,8,4,4,4]{3,6,5,4,2,1,0:T(4,128)}, u32[]{:S(2)}) %copy-start.3) | copy-done | bytes 2072
  4.2 0.0 copy-start.4
  4.2 0.7 %copy-done.4 = s32[1,1,1,8,4,3]{3,4,5,2,1,0:T(4,128)S(1)} copy-done((s32[1,1,1,8,4,3]{3,4,5,2,1,0:T(4,128)S(1)}, s32[1,1,1,8,4,3]{3,4,5,2,1,0:T(4,128)}, u32[]{:S(2)}) %copy-start.4) | copy-done | bytes 408
  4.9 0.0 copy-start.5
  4.9 0.7 %copy-done.5 = s32[1,1,1,8]{3,2,1,0:T(1,128)S(1)} copy-done((s32[1,1,1,8]{3,2,1,0:T(1,128)S(1)}, s32[1,1,1,8]{3,2,1,0:T(1,128)}, u32[]{:S(2)}) %copy-start.5) | copy-done | bytes 56
  5.6 27.2 %shard_map.64 = f32[2,16,16,128]{3,2,1,0:T(8,128)S(1)} custom-call(f32[2,16,16,128]{3,2,1,0:T(8,128)S(1)} %copy-done.1, f32[16,16,128]{2,1,0:T(8,128)S(1)} %copy-done.2, f32[4096,128]{1,0:T(8,128)S(1)} %bitcast.12, f32[4,4,4,8]{3,2,1,0:T(4,128)S(1)} %bitcast.13, s32[3,4,8]{2,1,0:T(4,128)S(1)} %bitcast.14, s32[8]{0:T(128)S(1)} %bitcast.15), custom_call_target="tpu_custom_call" | custom-call | tf_op jit(solution)/shard_map/pallas_call | solution.py:304
  32.8 0.7 %copy.9 = f32[2,16,16,128]{3,2,1,0:T(8,128)} copy(f32[2,16,16,128]{3,2,1,0:T(8,128)S(1)} %shard_map.64) | data formatting | bytes 524288
Async XLA Ops:
  0.0 1.6 %copy-start = (f32[1,1,1,8,4,4,4096]{6,5,4,3,2,1,0:T(4,128)S(1)}, f32[1,1,1,8,4,4,4096]{6,5,4,3,2,1,0:T(4,128)}, u32[]{:S(2)}) copy-start(f32[1,1,1,8,4,4,4096]{6,5,4,3,2,1,0:T(4,128)} %param.8) | copy-start | bytes 6291460
  1.6 0.9 %copy-start.1 = (f32[2,16,16,128]{3,2,1,0:T(8,128)S(1)}, f32[2,16,16,128]{3,2,1,0:T(8,128)}, u32[]{:S(2)}) copy-start(f32[2,16,16,128]{3,2,1,0:T(8,128)} %x_hbm.1) | copy-start | bytes 786436
  2.5 0.9 %copy-start.2 = (f32[16,16,128]{2,1,0:T(8,128)S(1)}, f32[16,16,128]{2,1,0:T(8,128)}, u32[]{:S(2)}) copy-start(f32[16,16,128]{2,1,0:T(8,128)} %pot_hbm.1) | copy-start | bytes 393220
  3.4 0.8 %copy-start.3 = (f32[1,1,1,8,4,4,4]{3,6,5,4,2,1,0:T(4,128)S(1)}, f32[1,1,1,8,4,4,4]{3,6,5,4,2,1,0:T(4,128)}, u32[]{:S(2)}) copy-start(f32[1,1,1,8,4,4,4]{3,6,5,4,2,1,0:T(4,128)} %param.9) | copy-start | bytes 6148
  4.2 0.7 %copy-start.4 = (s32[1,1,1,8,4,3]{3,4,5,2,1,0:T(4,128)S(1)}, s32[1,1,1,8,4,3]{3,4,5,2,1,0:T(4,128)}, u32[]{:S(2)}) copy-start(s32[1,1,1,8,4,3]{3,4,5,2,1,0:T(4,128)} %param.10) | copy-start | bytes 1156
  4.9 0.7 %copy-start.5 = (s32[1,1,1,8]{3,2,1,0:T(1,128)S(1)}, s32[1,1,1,8]{3,2,1,0:T(1,128)}, u32[]{:S(2)}) copy-start(s32[1,1,1,8]{3,2,1,0:T(1,128)} %param.11) | copy-start | bytes 100
where the time goes:
time: 34 us; the launch traced here: 33.5 us
  Pallas kernels  27.2 us (80%)
  local copies, waits for them, and re-layouts  6.25 us (18%)
    pallas_call x1, Pallas kernels, on_device(): pl.pallas_call(functools.partial(kernel, sizes), out_shape=jax.ShapeDtype...  27.2 us
    unnamed x13, local copies, waits for them, and re-layouts  6.25 us

commit v1 on v0

--- a/solution.py
+++ b/solution.py
@@ -19,7 +19,6 @@
     2.0 / 1925.0,
     -1.0 / 16632.0,
 ]
-PAD = 40
 
 
 def iota(shape, dim):
@@ -34,24 +33,16 @@
     return out
 
 
-def shear(v, back):
-    axis = v.ndim - 1
-    sub = iota(v.shape, axis - 1)
-    for bit in (1, 2, 4):
-        turn = (128 - 16 * bit) if back else 16 * bit
-        v = jnp.where((sub & bit) != 0, pltpu.roll(v, turn, axis), v)
-    return v
-
-
 def residues(n):
     return [0, 1] if n == 2 else [0, 1, n - 1]
 
 
 def kernel(
     sizes,
-    x_hbm, pot_hbm, p_hbm, cpl_ref, st_ref, cnt_ref,
+    x_hbm, pot_hbm, p_hbm, cpl_hbm, st_hbm, cnt_hbm,
     out_ref,
-    xpad, xe, ye, pot, pv, pr, sheared, accs, zs, zr, recv, zc, wrep, cs, mprime,
+    xt, xe, ye, pot, pv, pr, sheared, accs, zs, zr, recv, zc, wrep, cs, mprime, fold,
+    cpl_ref, st_ref, cnt_ref,
     lsem, hsend, hrecv, psend, precv,
 ):
     names = ("gx", "gy", "gz")
@@ -73,8 +64,14 @@
     load_y = pltpu.make_async_copy(x_hbm, ye.at[:, :, 8:24], lsem.at[1])
     load_p = pltpu.make_async_copy(p_hbm, pv, lsem.at[2])
     load_pot = pltpu.make_async_copy(pot_hbm, pot, lsem.at[3])
+    load_st = pltpu.make_async_copy(st_hbm, st_ref, lsem.at[4])
+    load_cnt = pltpu.make_async_copy(cnt_hbm, cnt_ref, lsem.at[5])
+    load_cpl = pltpu.make_async_copy(cpl_hbm, cpl_ref, lsem.at[6])
+    load_st.start()
+    load_p.start()
     load_x.start()
-    load_p.start()
+    load_cpl.start()
+    load_cnt.start()
     load_y.start()
     load_pot.start()
 
@@ -85,12 +82,49 @@
 
     def clear(i, carry):
         for b in range(2):
-            xpad[b, i] = jnp.zeros((48, 128), F32)
+            xt[b, i] = jnp.zeros((48, 128), F32)
         return carry
 
     lax.fori_loop(0, 48, clear, 0)
-    for b in range(2):
-        zc[b] = jnp.zeros((112, 128), F32)
+
+    def clear_mix(i, carry):
+        zc[i] = jnp.zeros((48, 128), F32)
+        return carry
+
+    lax.fori_loop(0, 48, clear_mix, 0)
+
+    def clear_sum(i, carry):
+        for b in range(2):
+            sheared[b, i] = jnp.zeros((16, 128), F32)
+        return carry
+
+    lax.fori_loop(0, 16, clear_sum, 0)
+
+    lane = iota((8, 128), 1)
+
+    def place(o, s):
+        a = st_ref[0, s, o] - 16 * (o >> 2)
+        b0 = st_ref[1, s, o] - 16 * ((o >> 1) & 1)
+        c = st_ref[2, s, o] - 128 * (o & 1)
+        return a, b0, c
+
+    load_st.wait()
+    load_cnt.wait()
+    load_p.wait()
+
+    def turn(o, carry):
+        for s in range(4):
+            n = o * 4 + s
+            _, b0, c = place(o, s)
+            by = (c + 16 * b0) & 127
+            for i in range(4):
+                for yh in range(2):
+                    plane = pv[pl.ds(n * 128 + yh * 4 + i, 16, stride=8), :]
+                    pr[pl.ds(n * 128 + i * 32 + yh * 16, 16), :] = pltpu.roll(plane, by, 1)
+        return carry
+
+    lax.fori_loop(0, 8, turn, 0)
+    load_cpl.wait()
 
     for s in range(4):
         for i in range(4):
@@ -126,57 +160,39 @@
 
     load_x.wait()
 
-    def lay(x, carry):
-        for b in range(2):
-            xpad[b, 16 + x, 16:32, :] = shear(xe[b, 6 + x], False)
-            sheared[b, x] = jnp.zeros((16, 128), F32)
-        return carry
-
-    lax.fori_loop(0, 16, lay, 0)
     flat = xe[:, 6:22].reshape(512, 128)
+    fold[...] = flat
+    for b in range(2):
+        for y in range(16):
+            plane = fold[pl.ds(b * 256 + y, 16, stride=16), :]
+            xt[b, 16 + y, 16:32, :] = pltpu.roll(plane, 16 * (y % 8), 1) if y % 8 else plane
     row, col = iota((16, 128), 0), iota((16, 128), 1)
     sel = (col == jnp.where(row < 8, 120 + row, row - 8)).astype(F32)
     zs[...] = lax.dot_general(sel, flat, (((1,), (1,)), ((), ())), precision=HI,
                               preferred_element_type=F32)
     send(zs.at[0:8], zr.at[0:8], 4, (0, 0, 1))
     send(zs.at[8:16], zr.at[8:16], 5, (0, 0, -1))
-    load_p.wait()
-
-    lane, sub = iota((8, 128), 1), iota((8, 128), 0)
-
-    def place(n):
+    def gather(n, carry):
         o, s = n >> 2, n & 3
-        a = st_ref[0, s, o] - 16 * (o >> 2)
-        b0 = st_ref[1, s, o] - 16 * ((o >> 1) & 1)
-        c = st_ref[2, s, o] - 128 * (o & 1)
-        return o, s, a, b0, c
-
-    def turn(n, carry):
-        _, _, _, b0, c = place(n)
-        by = (c + 16 * b0) & 127
-        for i in range(4):
-            plane = pv[pl.ds(n * 128 + i, 32, stride=4), :]
-            pr[pl.ds(n * 128 + i * 32, 32), :] = pltpu.roll(plane, by, 1)
-        return carry
-
-    lax.fori_loop(0, 32, turn, 0)
-
-    def gather(n, carry):
-        _, _, a, b0, c = place(n)
-        z = (lane - 16 * (sub + b0)) & 127
-        keep = (z >= c) & (z < c + 16)
+        a, b0, c = place(o, s)
+        keep = []
+        for y in range(8):
+            z = (lane - 16 * (y + b0)) & 127
+            keep.append((z >= c) & (z < c + 16))
         acc = [jnp.zeros((8, 128), F32) for _ in range(8)]
-        for x in range(16):
-            for yh in range(2):
-                rows = [
-                    jnp.broadcast_to(pr[pl.ds(n * 128 + i * 32 + x * 2 + yh, 1), :], (8, 128))
-                    for i in range(4)
-                ]
+        for yh in range(2):
+            for h in range(2):
+                g = []
                 for b in range(2):
-                    g = xpad[b, 16 + a + x, pl.ds(16 + b0 + 8 * yh, 8), :]
-                    g = jnp.where(keep, g, 0.0)
-                    for i in range(4):
-                        acc[b * 4 + i] = acc[b * 4 + i] + g * rows[i]
+                    v = jnp.zeros((8, 128), F32)
+                    for y in range(8):
+                        w = xt[b, 16 + b0 + 8 * yh + y, pl.ds(16 + a + 8 * h, 8), :]
+                        v = jnp.where(keep[y], w, v)
+                    g.append(v)
+                for i in range(4):
+                    p = pr[pl.ds(n * 128 + i * 32 + yh * 16 + h * 8, 8), :]
+                    for b in range(2):
+                        acc[b * 4 + i] = acc[b * 4 + i] + g[b] * p
         for k in range(8):
             accs[pl.ds(n * 64 + k * 8, 8), :] = acc[k]
         return carry
@@ -203,24 +219,25 @@
     load_pot.wait()
     r128, c128 = iota((128, 128), 0), iota((128, 128), 1)
     near = jnp.where(r128 == c128, -0.5 * 3.0 * COEFF[0], band(r128 - c128))
-    out_ref[...] = lax.dot_general(flat, near, (((1,), (0,)), ((), ())), precision=HI,
-                                   preferred_element_type=F32).reshape(2, 16, 16, 128)
+    base = lax.dot_general(flat, near, (((1,), (0,)), ((), ())), precision=HI,
+                           preferred_element_type=F32)
     for copy in sends:
         copy.wait()
     far = band(jnp.where(row < 8, row - 8, 120 + row) - col)
     edge = lax.dot_general(zr[...], far, (((0,), (0,)), ((), ())), precision=HI,
-                           preferred_element_type=F32).reshape(2, 16, 16, 128)
-    out_ref[...] += edge
+                           preferred_element_type=F32)
+    out_ref[...] = base + edge
 
     def stencil(x, carry):
         for b in range(2):
-            acc = pot[x] * xe[b, x + 6] + out_ref[b, x]
+            here = pl.ds(b * 256 + x * 16, 16)
+            acc = pot[x] * xe[b, x + 6] + out_ref[here, :]
             for k in range(1, 7):
                 four = (ye[b, x, 8 - k : 24 - k, :] + ye[b, x, 8 + k : 24 + k, :]) + (
                     xe[b, x + 6 - k] + xe[b, x + 6 + k]
                 )
                 acc = acc + (-0.5 * COEFF[k]) * four
-            out_ref[b, x] = acc
+            out_ref[here, :] = acc
         return carry
 
     lax.fori_loop(0, 16, stencil, 0)
@@ -251,40 +268,43 @@
                                 (((1,), (0,)), ((), ())), precision=HI,
                                 preferred_element_type=F32)
 
-    def scatter(n, carry):
-        o, s, a, b0, c = place(n)
-        live = jnp.where(s < cnt_ref[o], 1.0, 0.0).astype(F32)
-        planes = [pr[pl.ds(n * 128 + i * 32, 32), :] for i in range(4)]
-        for b in range(2):
-            mix = jnp.zeros((32, 128), F32)
-            for i in range(4):
-                mix = mix + planes[i] * (wrep[pl.ds(n * 8 + b * 4 + i, 1), :] * live)
-            zc[b, PAD : PAD + 32, :] = mix
-        low = b0 >> 3
-        rest = b0 & 7
-        first = sub >= rest
-        z = (lane - 16 * sub) & 127
-        window = (z >= c) & (z < c + 16)
-        for t in range(2):
-            y = 8 * t + sub - b0
-            keep = window & (y >= 0) & (y < 16)
-            start = PAD - 2 * a + t - low
-            for x in range(16):
+    def scatter(o, carry):
+        spots = []
+        for s in range(4):
+            n = o * 4 + s
+            live = jnp.where(s < cnt_ref[o], 1.0, 0.0).astype(F32)
+            for b in range(2):
+                mix = jnp.zeros((32, 128), F32)
+                for i in range(4):
+                    plane = pr[pl.ds(n * 128 + i * 32, 32), :]
+                    mix = mix + plane * (wrep[pl.ds(n * 8 + b * 4 + i, 1), :] * live)
+                for yh in range(2):
+                    zc[s * 12 + b * 6 + 2 + yh, 16:32, :] = mix[yh * 16 : yh * 16 + 16]
+            spots.append(place(o, s))
+        for r in range(8):
+            keep = []
+            z = (lane - 16 * r) & 127
+            for a, b0, c in spots:
+                keep.append((z >= c) & (z < c + 16))
+            for y in (r, r + 8):
                 for b in range(2):
-                    one = jnp.broadcast_to(zc[b, pl.ds(start + 2 * x, 1), :], (8, 128))
-                    two = jnp.broadcast_to(zc[b, pl.ds(start + 2 * x - 1, 1), :], (8, 128))
-                    v = jnp.where(first, one, two)
-                    sheared[b, x, 8 * t : 8 * t + 8, :] += jnp.where(keep, v, 0.0)
-        return carry
-
-    lax.fori_loop(0, 32, scatter, 0)
-
-    def finish(x, carry):
-        for b in range(2):
-            out_ref[b, x] += shear(sheared[b, x], True)
-        return carry
-
-    lax.fori_loop(0, 16, finish, 0)
+                    for h in range(2):
+                        acc = sheared[b, y, 8 * h : 8 * h + 8, :]
+                        for s, (a, b0, c) in enumerate(spots):
+                            w = zc[s * 12 + b * 6 + 2 + ((y - b0) >> 3),
+                                   pl.ds(16 - a + 8 * h, 8), :]
+                            acc = acc + jnp.where(keep[s], w, 0.0)
+                        sheared[b, y, 8 * h : 8 * h + 8, :] = acc
+        return carry
+
+    lax.fori_loop(0, 8, scatter, 0)
+
+    for b in range(2):
+        for y in range(16):
+            plane = sheared[b, y]
+            if y % 8:
+                plane = pltpu.roll(plane, 128 - 16 * (y % 8), 1)
+            out_ref[pl.ds(b * 256 + y, 16, stride=16), :] += plane
 
 
 def solution(mesh):
@@ -298,13 +318,12 @@
         matrices = coupling.reshape(8, 4, 4, 4).transpose(1, 2, 3, 0)
         starts = block_starts.reshape(8, 4, 3).transpose(2, 1, 0)
         counts = owner_counts.reshape(8)
-        anyspace = pl.BlockSpec(memory_space=pl.ANY)
+        hbm = pl.BlockSpec(memory_space=pltpu.HBM)
         vmem = pl.BlockSpec(memory_space=pltpu.VMEM)
-        smem = pl.BlockSpec(memory_space=pltpu.SMEM)
         return pl.pallas_call(
             functools.partial(kernel, sizes),
-            out_shape=jax.ShapeDtypeStruct((2, 16, 16, 128), F32),
-            in_specs=[anyspace, anyspace, anyspace, vmem, smem, smem],
+            out_shape=jax.ShapeDtypeStruct((512, 128), F32),
+            in_specs=[hbm] * 6,
             out_specs=vmem,
             scratch_shapes=[
                 pltpu.VMEM((2, 48, 48, 128), F32),
@@ -318,20 +337,24 @@
                 pltpu.VMEM((16, 512), F32),
                 pltpu.VMEM((16, 512), F32),
                 pltpu.VMEM((nslots, 1, 256), F32),
-                pltpu.VMEM((2, 112, 128), F32),
+                pltpu.VMEM((48, 48, 128), F32),
                 pltpu.VMEM((256, 128), F32),
                 pltpu.VMEM((64, 8), F32),
                 pltpu.VMEM((256, 256), F32),
-                pltpu.SemaphoreType.DMA((4,)),
+                pltpu.VMEM((512, 128), F32),
+                pltpu.VMEM((4, 4, 4, 8), F32),
+                pltpu.SMEM((3, 4, 8), jnp.int32),
+                pltpu.SMEM((8,), jnp.int32),
+                pltpu.SemaphoreType.DMA((7,)),
                 pltpu.SemaphoreType.DMA((6,)),
                 pltpu.SemaphoreType.DMA((6,)),
                 pltpu.SemaphoreType.DMA((nslots,)),
                 pltpu.SemaphoreType.DMA((nslots,)),
             ],
             compiler_params=pltpu.CompilerParams(
-                collective_id=0, has_side_effects=True, vmem_limit_bytes=32 * 1024 * 1024
+                collective_id=0, has_side_effects=True, vmem_limit_bytes=60 * 1024 * 1024
             ),
-        )(orbitals, potential, rows, matrices, starts, counts)
+        )(orbitals, potential, rows, matrices, starts, counts).reshape(2, 16, 16, 128)
 
     in_specs = (
         P(None, "gx", "gy", "gz"),

time: 34 us -> 21.6 us (0.64)
  Pallas kernels: 27.2 us -> 19.7 us
  local copies, waits for them, and re-layouts: 6.25 us -> 1.67 us
    pallas_call x1, Pallas kernels: 27.2 us -> 19.7 us  [on_device(): pl.pallas_call(functools.partial(kernel, sizes), out_shape=jax.ShapeDtype...]
    unnamed x13 -> x1, local copies, waits for them, and re-layouts: 6.25 us -> 1.67 us
where the time goes in v1:
time: 21.6 us; the launch traced here: 21.4 us
  Pallas kernels  19.7 us (91%)
  local copies, waits for them, and re-layouts  1.67 us (8%)
    pallas_call x1, Pallas kernels, on_device(): pl.pallas_call(functools.partial(kernel, sizes), out_shape=jax.ShapeDtype...  19.7 us
    unnamed x1, local copies, waits for them, and re-layouts  1.67 us

profile of v1, /device:TPU:0, one launch (start us, length us, event | category | flops | bytes accessed | tf_op | source)
XLA Modules:
  0.0 21.4 jit_solution(2867021653853456431)
XLA Ops:
  0.0 19.7 %shard_map.64 = f32[512,128]{1,0:T(8,128)} custom-call(f32[2,16,16,128]{3,2,1,0:T(8,128)} %x_hbm.1, f32[16,16,128]{2,1,0:T(8,128)} %pot_hbm.1, f32[4096,128]{1,0:T(8,128)} %bitcast.13, f32[4,4,4,8]{3,2,1,0:T(4,128)} %bitcast.15, s32[3,4,8]{2,1,0:T(4,128)} %bitcast.16, s32[8]{0:T(128)} %bitcast.17), custom_call_target="tpu_custom_call" | custom-call | tf_op jit(solution)/shard_map/pallas_call | solution.py:323
  19.7 1.7 %copy.9 = f32[2,16,16,128]{3,2,1,0:T(8,128)} copy(f32[2,16,16,128]{3,2,1,0:T(8,128)} %bitcast.14) | data formatting | bytes 524288

commit v2 on v1

--- a/solution.py
+++ b/solution.py
@@ -108,22 +108,15 @@
         c = st_ref[2, s, o] - 128 * (o & 1)
         return a, b0, c
 
-    load_st.wait()
-    load_cnt.wait()
-    load_p.wait()
-
-    def turn(o, carry):
-        for s in range(4):
-            n = o * 4 + s
-            _, b0, c = place(o, s)
-            by = (c + 16 * b0) & 127
-            for i in range(4):
-                for yh in range(2):
-                    plane = pv[pl.ds(n * 128 + yh * 4 + i, 16, stride=8), :]
-                    pr[pl.ds(n * 128 + i * 32 + yh * 16, 16), :] = pltpu.roll(plane, by, 1)
-        return carry
-
-    lax.fori_loop(0, 8, turn, 0)
+    load_x.wait()
+
+    fold[...] = xe[:, 6:22].reshape(512, 128)
+    for b in range(2):
+        planes = [fold[pl.ds(b * 256 + y, 16, stride=16), :] for y in range(16)]
+        planes = [pltpu.roll(v, 16 * (y % 8), 1) if y % 8 else v for y, v in enumerate(planes)]
+        for y, v in enumerate(planes):
+            xt[b, 16 + y, 16:32, :] = v
+
     load_cpl.wait()
 
     for s in range(4):
@@ -158,20 +151,24 @@
     send(x_hbm.at[:, 10:16], xe.at[:, 0:6], 2, (1, 0, 0))
     send(x_hbm.at[:, 0:6], xe.at[:, 22:28], 3, (-1, 0, 0))
 
-    load_x.wait()
-
-    flat = xe[:, 6:22].reshape(512, 128)
-    fold[...] = flat
-    for b in range(2):
-        for y in range(16):
-            plane = fold[pl.ds(b * 256 + y, 16, stride=16), :]
-            xt[b, 16 + y, 16:32, :] = pltpu.roll(plane, 16 * (y % 8), 1) if y % 8 else plane
-    row, col = iota((16, 128), 0), iota((16, 128), 1)
-    sel = (col == jnp.where(row < 8, 120 + row, row - 8)).astype(F32)
-    zs[...] = lax.dot_general(sel, flat, (((1,), (1,)), ((), ())), precision=HI,
-                              preferred_element_type=F32)
-    send(zs.at[0:8], zr.at[0:8], 4, (0, 0, 1))
-    send(zs.at[8:16], zr.at[8:16], 5, (0, 0, -1))
+    load_st.wait()
+    load_cnt.wait()
+    load_p.wait()
+
+    def turn(o, carry):
+        for s in range(4):
+            n = o * 4 + s
+            _, b0, c = place(o, s)
+            by = (c + 16 * b0) & 127
+            planes = [
+                pltpu.roll(pv[pl.ds(n * 128 + yh * 4 + i, 16, stride=8), :], by, 1)
+                for i in range(4) for yh in range(2)
+            ]
+            for k, plane in enumerate(planes):
+                pr[pl.ds(n * 128 + k * 16, 16), :] = plane
+        return carry
+
+    lax.fori_loop(0, 8, turn, 0)
     def gather(n, carry):
         o, s = n >> 2, n & 3
         a, b0, c = place(o, s)
@@ -215,11 +212,17 @@
         copy.start()
         parts.append(copy)
 
+    row, col = iota((16, 128), 0), iota((16, 128), 1)
+    sel = (col == jnp.where(row < 8, 120 + row, row - 8)).astype(F32)
+    zs[...] = lax.dot_general(sel, fold[...], (((1,), (1,)), ((), ())), precision=HI,
+                              preferred_element_type=F32)
+    send(zs.at[0:8], zr.at[0:8], 4, (0, 0, 1))
+    send(zs.at[8:16], zr.at[8:16], 5, (0, 0, -1))
     load_y.wait()
     load_pot.wait()
     r128, c128 = iota((128, 128), 0), iota((128, 128), 1)
     near = jnp.where(r128 == c128, -0.5 * 3.0 * COEFF[0], band(r128 - c128))
-    base = lax.dot_general(flat, near, (((1,), (0,)), ((), ())), precision=HI,
+    base = lax.dot_general(fold[...], near, (((1,), (0,)), ((), ())), precision=HI,
                            preferred_element_type=F32)
     for copy in sends:
         copy.wait()
@@ -229,6 +232,7 @@
     out_ref[...] = base + edge
 
     def stencil(x, carry):
+        done = []
         for b in range(2):
             here = pl.ds(b * 256 + x * 16, 16)
             acc = pot[x] * xe[b, x + 6] + out_ref[here, :]
@@ -237,7 +241,9 @@
                     xe[b, x + 6 - k] + xe[b, x + 6 + k]
                 )
                 acc = acc + (-0.5 * COEFF[k]) * four
-            out_ref[here, :] = acc
+            done.append(acc)
+        for b in range(2):
+            out_ref[pl.ds(b * 256 + x * 16, 16), :] = done[b]
         return carry
 
     lax.fori_loop(0, 16, stencil, 0)
@@ -269,7 +275,7 @@
                                 preferred_element_type=F32)
 
     def scatter(o, carry):
-        spots = []
+        spots, mixes = [], []
         for s in range(4):
             n = o * 4 + s
             live = jnp.where(s < cnt_ref[o], 1.0, 0.0).astype(F32)
@@ -278,33 +284,39 @@
                 for i in range(4):
                     plane = pr[pl.ds(n * 128 + i * 32, 32), :]
                     mix = mix + plane * (wrep[pl.ds(n * 8 + b * 4 + i, 1), :] * live)
-                for yh in range(2):
-                    zc[s * 12 + b * 6 + 2 + yh, 16:32, :] = mix[yh * 16 : yh * 16 + 16]
+                mixes.append(mix)
             spots.append(place(o, s))
+        for k, mix in enumerate(mixes):
+            for yh in range(2):
+                zc[k * 6 + 2 + yh, 16:32, :] = mix[yh * 16 : yh * 16 + 16]
         for r in range(8):
             keep = []
             z = (lane - 16 * r) & 127
             for a, b0, c in spots:
                 keep.append((z >= c) & (z < c + 16))
-            for y in (r, r + 8):
-                for b in range(2):
-                    for h in range(2):
-                        acc = sheared[b, y, 8 * h : 8 * h + 8, :]
-                        for s, (a, b0, c) in enumerate(spots):
-                            w = zc[s * 12 + b * 6 + 2 + ((y - b0) >> 3),
-                                   pl.ds(16 - a + 8 * h, 8), :]
-                            acc = acc + jnp.where(keep[s], w, 0.0)
-                        sheared[b, y, 8 * h : 8 * h + 8, :] = acc
+            where = [(b, y, h) for y in (r, r + 8) for b in range(2) for h in range(2)]
+            sums = []
+            for b, y, h in where:
+                acc = sheared[b, y, 8 * h : 8 * h + 8, :]
+                for s, (a, b0, c) in enumerate(spots):
+                    w = zc[s * 12 + b * 6 + 2 + ((y - b0) >> 3), pl.ds(16 - a + 8 * h, 8), :]
+                    acc = acc + jnp.where(keep[s], w, 0.0)
+                sums.append(acc)
+            for (b, y, h), acc in zip(where, sums):
+                sheared[b, y, 8 * h : 8 * h + 8, :] = acc
         return carry
 
     lax.fori_loop(0, 8, scatter, 0)
 
     for b in range(2):
-        for y in range(16):
-            plane = sheared[b, y]
-            if y % 8:
-                plane = pltpu.roll(plane, 128 - 16 * (y % 8), 1)
-            out_ref[pl.ds(b * 256 + y, 16, stride=16), :] += plane
+        planes = [sheared[b, y] for y in range(16)]
+        planes = [
+            (pltpu.roll(v, 128 - 16 * (y % 8), 1) if y % 8 else v)
+            + out_ref[pl.ds(b * 256 + y, 16, stride=16), :]
+            for y, v in enumerate(planes)
+        ]
+        for y, v in enumerate(planes):
+            out_ref[pl.ds(b * 256 + y, 16, stride=16), :] = v
 
 
 def solution(mesh):

time: 21.6 us -> 21.6 us (level)
  no operation moved by 1% of the time
where the time goes in v2:
time: 21.6 us; the launch traced here: 21.4 us
  Pallas kernels  19.7 us (91%)
  local copies, waits for them, and re-layouts  1.67 us (8%)
    pallas_call x1, Pallas kernels, on_device(): pl.pallas_call(functools.partial(kernel, sizes), out_shape=jax.ShapeDtype...  19.7 us
    unnamed x1, local copies, waits for them, and re-layouts  1.67 us

profile of v2, /device:TPU:0, one launch (start us, length us, event | category | flops | bytes accessed | tf_op | source)
XLA Modules:
  0.0 21.4 jit_solution(15347230285935688471)
XLA Ops:
  0.0 19.7 %shard_map.64 = f32[512,128]{1,0:T(8,128)} custom-call(f32[2,16,16,128]{3,2,1,0:T(8,128)} %x_hbm.1, f32[16,16,128]{2,1,0:T(8,128)} %pot_hbm.1, f32[4096,128]{1,0:T(8,128)} %bitcast.13, f32[4,4,4,8]{3,2,1,0:T(4,128)} %bitcast.15, s32[3,4,8]{2,1,0:T(4,128)} %bitcast.16, s32[8]{0:T(128)} %bitcast.17), custom_call_target="tpu_custom_call" | custom-call | tf_op jit(solution)/shard_map/pallas_call | solution.py:335
  19.7 1.7 %copy.9 = f32[2,16,16,128]{3,2,1,0:T(8,128)} copy(f32[2,16,16,128]{3,2,1,0:T(8,128)} %bitcast.14) | data formatting | bytes 524288

commit v3 on v2

--- a/solution.py
+++ b/solution.py
@@ -62,13 +62,18 @@
 
     load_x = pltpu.make_async_copy(x_hbm, xe.at[:, 6:22], lsem.at[0])
     load_y = pltpu.make_async_copy(x_hbm, ye.at[:, :, 8:24], lsem.at[1])
-    load_p = pltpu.make_async_copy(p_hbm, pv, lsem.at[2])
+    load_p = [
+        pltpu.make_async_copy(p_hbm.at[pl.ds(k * 1024, 1024)], pv.at[pl.ds(k * 1024, 1024)],
+                              lsem.at[7 + k])
+        for k in range(4)
+    ]
     load_pot = pltpu.make_async_copy(pot_hbm, pot, lsem.at[3])
     load_st = pltpu.make_async_copy(st_hbm, st_ref, lsem.at[4])
     load_cnt = pltpu.make_async_copy(cnt_hbm, cnt_ref, lsem.at[5])
     load_cpl = pltpu.make_async_copy(cpl_hbm, cpl_ref, lsem.at[6])
     load_st.start()
-    load_p.start()
+    for copy in load_p:
+        copy.start()
     load_x.start()
     load_cpl.start()
     load_cnt.start()
@@ -81,17 +86,16 @@
         pl.semaphore_signal(barrier, inc=1, device_id=device(e), device_id_type=MESH)
 
     def clear(i, carry):
-        for b in range(2):
-            xt[b, i] = jnp.zeros((48, 128), F32)
+        xt[pl.ds(i * 96, 96), :] = jnp.zeros((96, 128), F32)
         return carry
 
     lax.fori_loop(0, 48, clear, 0)
 
     def clear_mix(i, carry):
-        zc[i] = jnp.zeros((48, 128), F32)
-        return carry
-
-    lax.fori_loop(0, 48, clear_mix, 0)
+        zc[pl.ds(i * 96, 96), :] = jnp.zeros((96, 128), F32)
+        return carry
+
+    lax.fori_loop(0, 24, clear_mix, 0)
 
     def clear_sum(i, carry):
         for b in range(2):
@@ -115,24 +119,7 @@
         planes = [fold[pl.ds(b * 256 + y, 16, stride=16), :] for y in range(16)]
         planes = [pltpu.roll(v, 16 * (y % 8), 1) if y % 8 else v for y, v in enumerate(planes)]
         for y, v in enumerate(planes):
-            xt[b, 16 + y, 16:32, :] = v
-
-    load_cpl.wait()
-
-    for s in range(4):
-        for i in range(4):
-            cs[pl.ds((s * 4 + i) * 4, 4), :] = cpl_ref[s, i]
-    pick = (iota((256, 8), 0) // 32 == iota((256, 8), 1)).astype(F32)
-    per_row = lax.dot_general(pick, cs[...], (((1,), (1,)), ((), ())), precision=HI,
-                              preferred_element_type=F32)
-    r64, c64 = iota((256, 64), 0), iota((256, 64), 1)
-    own = ((r64 // 8) % 4 == c64 // 16) & (r64 % 4 == (c64 // 4) % 4)
-    per_row = jnp.where(own, per_row, 0.0)
-    spread = (iota((64, 256), 0) % 4 == iota((64, 256), 1) % 4).astype(F32)
-    wide = lax.dot_general(per_row, spread, (((1,), (0,)), ((), ())), precision=HI,
-                           preferred_element_type=F32)
-    same = iota((256, 256), 0) // 4 == iota((256, 256), 1) // 4
-    mprime[...] = jnp.where(same, wide, 0.0)
+            xt[b * 2304 + (16 + y) * 48 + 16 : b * 2304 + (16 + y) * 48 + 32, :] = v
 
     pl.semaphore_wait(barrier, len(others))
 
@@ -153,7 +140,6 @@
 
     load_st.wait()
     load_cnt.wait()
-    load_p.wait()
 
     def turn(o, carry):
         for s in range(4):
@@ -168,10 +154,14 @@
                 pr[pl.ds(n * 128 + k * 16, 16), :] = plane
         return carry
 
-    lax.fori_loop(0, 8, turn, 0)
+    for k in range(4):
+        load_p[k].wait()
+        lax.fori_loop(2 * k, 2 * k + 2, turn, 0)
+
     def gather(n, carry):
         o, s = n >> 2, n & 3
         a, b0, c = place(o, s)
+        corner = (16 + b0) * 48 + 16 + a
         keep = []
         for y in range(8):
             z = (lane - 16 * (y + b0)) & 127
@@ -183,7 +173,7 @@
                 for b in range(2):
                     v = jnp.zeros((8, 128), F32)
                     for y in range(8):
-                        w = xt[b, 16 + b0 + 8 * yh + y, pl.ds(16 + a + 8 * h, 8), :]
+                        w = xt[pl.ds(corner + (b * 2304 + (8 * yh + y) * 48 + 8 * h), 8), :]
                         v = jnp.where(keep[y], w, v)
                     g.append(v)
                 for i in range(4):
@@ -222,14 +212,10 @@
     load_pot.wait()
     r128, c128 = iota((128, 128), 0), iota((128, 128), 1)
     near = jnp.where(r128 == c128, -0.5 * 3.0 * COEFF[0], band(r128 - c128))
-    base = lax.dot_general(fold[...], near, (((1,), (0,)), ((), ())), precision=HI,
+    out_ref[...] = lax.dot_general(fold[...], near, (((1,), (0,)), ((), ())), precision=HI,
                            preferred_element_type=F32)
-    for copy in sends:
+    for copy in sends[:4]:
         copy.wait()
-    far = band(jnp.where(row < 8, row - 8, 120 + row) - col)
-    edge = lax.dot_general(zr[...], far, (((0,), (0,)), ((), ())), precision=HI,
-                           preferred_element_type=F32)
-    out_ref[...] = base + edge
 
     def stencil(x, carry):
         done = []
@@ -247,6 +233,31 @@
         return carry
 
     lax.fori_loop(0, 16, stencil, 0)
+
+    load_cpl.wait()
+
+    for s in range(4):
+        for i in range(4):
+            cs[pl.ds((s * 4 + i) * 4, 4), :] = cpl_ref[s, i]
+    pick = (iota((256, 8), 0) // 32 == iota((256, 8), 1)).astype(F32)
+    per_row = lax.dot_general(pick, cs[...], (((1,), (1,)), ((), ())), precision=HI,
+                              preferred_element_type=F32)
+    r64, c64 = iota((256, 64), 0), iota((256, 64), 1)
+    own = ((r64 // 8) % 4 == c64 // 16) & (r64 % 4 == (c64 // 4) % 4)
+    per_row = jnp.where(own, per_row, 0.0)
+    spread = (iota((64, 256), 0) % 4 == iota((64, 256), 1) % 4).astype(F32)
+    wide = lax.dot_general(per_row, spread, (((1,), (0,)), ((), ())), precision=HI,
+                           preferred_element_type=F32)
+    same = iota((256, 256), 0) // 4 == iota((256, 256), 1) // 4
+    mprime[...] = jnp.where(same, wide, 0.0)
+
+    for copy in sends[4:]:
+        copy.wait()
+    far = band(jnp.where(row < 8, row - 8, 120 + row) - col)
+    edge = lax.dot_general(zr[...], far, (((0,), (0,)), ((), ())), precision=HI,
+                           preferred_element_type=F32)
+    out_ref[...] += edge
+
 
     for copy in parts:
         copy.wait()
@@ -288,18 +299,23 @@
             spots.append(place(o, s))
         for k, mix in enumerate(mixes):
             for yh in range(2):
-                zc[k * 6 + 2 + yh, 16:32, :] = mix[yh * 16 : yh * 16 + 16]
+                zc[(k * 6 + 2 + yh) * 48 + 16 : (k * 6 + 2 + yh) * 48 + 32, :] = mix[yh * 16 : yh * 16 + 16]
         for r in range(8):
             keep = []
             z = (lane - 16 * r) & 127
             for a, b0, c in spots:
                 keep.append((z >= c) & (z < c + 16))
+            corner = {
+                (s, y): ((y - b0) >> 3) * 48 - a
+                for s, (a, b0, c) in enumerate(spots) for y in (r, r + 8)
+            }
             where = [(b, y, h) for y in (r, r + 8) for b in range(2) for h in range(2)]
             sums = []
             for b, y, h in where:
                 acc = sheared[b, y, 8 * h : 8 * h + 8, :]
-                for s, (a, b0, c) in enumerate(spots):
-                    w = zc[s * 12 + b * 6 + 2 + ((y - b0) >> 3), pl.ds(16 - a + 8 * h, 8), :]
+                for s in range(4):
+                    at = (s * 12 + b * 6 + 2) * 48 + 16 + 8 * h
+                    w = zc[pl.ds(corner[s, y] + at, 8), :]
                     acc = acc + jnp.where(keep[s], w, 0.0)
                 sums.append(acc)
             for (b, y, h), acc in zip(where, sums):
@@ -338,7 +354,7 @@
             in_specs=[hbm] * 6,
             out_specs=vmem,
             scratch_shapes=[
-                pltpu.VMEM((2, 48, 48, 128), F32),
+                pltpu.VMEM((4608, 128), F32),
                 pltpu.VMEM((2, 28, 16, 128), F32),
                 pltpu.VMEM((2, 16, 32, 128), F32),
                 pltpu.VMEM((16, 16, 128), F32),
@@ -349,7 +365,7 @@
                 pltpu.VMEM((16, 512), F32),
                 pltpu.VMEM((16, 512), F32),
                 pltpu.VMEM((nslots, 1, 256), F32),
-                pltpu.VMEM((48, 48, 128), F32),
+                pltpu.VMEM((2304, 128), F32),
                 pltpu.VMEM((256, 128), F32),
                 pltpu.VMEM((64, 8), F32),
                 pltpu.VMEM((256, 256), F32),
@@ -357,7 +373,7 @@
                 pltpu.VMEM((4, 4, 4, 8), F32),
                 pltpu.SMEM((3, 4, 8), jnp.int32),
                 pltpu.SMEM((8,), jnp.int32),
-                pltpu.SemaphoreType.DMA((7,)),
+                pltpu.SemaphoreType.DMA((11,)),
                 pltpu.SemaphoreType.DMA((6,)),
                 pltpu.SemaphoreType.DMA((6,)),
                 pltpu.SemaphoreType.DMA((nslots,)),

time: 21.6 us -> 21.6 us (level)
  no operation moved by 1% of the time
where the time goes in v3:
time: 21.6 us; the launch traced here: 21.4 us
  Pallas kernels  19.7 us (91%)
  local copies, waits for them, and re-layouts  1.67 us (8%)
    pallas_call x1, Pallas kernels, on_device(): pl.pallas_call(functools.partial(kernel, sizes), out_shape=jax.ShapeDtype...  19.7 us
    unnamed x1, local copies, waits for them, and re-layouts  1.67 us

profile of v3, /device:TPU:0, one launch (start us, length us, event | category | flops | bytes accessed | tf_op | source)
XLA Modules:
  0.0 21.4 jit_solution(4480900712753476089)
XLA Ops:
  0.0 19.7 %shard_map.64 = f32[512,128]{1,0:T(8,128)} custom-call(f32[2,16,16,128]{3,2,1,0:T(8,128)} %x_hbm.1, f32[16,16,128]{2,1,0:T(8,128)} %pot_hbm.1, f32[4096,128]{1,0:T(8,128)} %bitcast.13, f32[4,4,4,8]{3,2,1,0:T(4,128)} %bitcast.15, s32[3,4,8]{2,1,0:T(4,128)} %bitcast.16, s32[8]{0:T(128)} %bitcast.17), custom_call_target="tpu_custom_call" | custom-call | tf_op jit(solution)/shard_map/pallas_call | solution.py:351
  19.7 1.7 %copy.9 = f32[2,16,16,128]{3,2,1,0:T(8,128)} copy(f32[2,16,16,128]{3,2,1,0:T(8,128)} %bitcast.14) | data formatting | bytes 524288

commit v4 on v3

--- a/solution.py
+++ b/solution.py
@@ -33,6 +33,24 @@
     return out
 
 
+def split3(v):
+    hi = v.astype(jnp.bfloat16)
+    left = v - hi.astype(F32)
+    mid = left.astype(jnp.bfloat16)
+    low = (left - mid.astype(F32)).astype(jnp.bfloat16)
+    return hi, mid, low
+
+
+def exact_dot(v, units, dims, flip=False):
+    units = units.astype(jnp.bfloat16)
+    total = None
+    for term in reversed(split3(v)):
+        pair = (units, term) if flip else (term, units)
+        out = lax.dot_general(*pair, (dims, ((), ())), preferred_element_type=F32)
+        total = out if total is None else total + out
+    return total
+
+
 def residues(n):
     return [0, 1] if n == 2 else [0, 1, n - 1]
 
@@ -40,8 +58,8 @@
 def kernel(
     sizes,
     x_hbm, pot_hbm, p_hbm, cpl_hbm, st_hbm, cnt_hbm,
-    out_ref,
-    xt, xe, ye, pot, pv, pr, sheared, accs, zs, zr, recv, zc, wrep, cs, mprime, fold,
+    out_hbm,
+    base, xt, xe, ye, pot, pv, pr, sheared, accs, zs, zr, recv, zc, wrep, cs, mprime, fold,
     cpl_ref, st_ref, cnt_ref,
     lsem, hsend, hrecv, psend, precv,
 ):
@@ -82,6 +100,7 @@
 
     barrier = pltpu.get_barrier_semaphore()
     others = [e for e in slots if e != (0, 0, 0)]
+    others.sort(key=lambda e: -sum(e))
     for e in others:
         pl.semaphore_signal(barrier, inc=1, device_id=device(e), device_id_type=MESH)
 
@@ -121,6 +140,9 @@
         for y, v in enumerate(planes):
             xt[b * 2304 + (16 + y) * 48 + 16 : b * 2304 + (16 + y) * 48 + 32, :] = v
 
+    row, col = iota((16, 128), 0), iota((16, 128), 1)
+    sel = (col == jnp.where(row < 8, 120 + row, row - 8)).astype(F32)
+    zs[...] = exact_dot(fold[...], sel, ((1,), (1,)), flip=True)
     pl.semaphore_wait(barrier, len(others))
 
     sends = []
@@ -137,60 +159,59 @@
     send(x_hbm.at[:, :, 0:8, :], ye.at[:, :, 24:32, :], 1, (0, -1, 0))
     send(x_hbm.at[:, 10:16], xe.at[:, 0:6], 2, (1, 0, 0))
     send(x_hbm.at[:, 0:6], xe.at[:, 22:28], 3, (-1, 0, 0))
+    send(zs.at[0:8], zr.at[0:8], 4, (0, 0, 1))
+    send(zs.at[8:16], zr.at[8:16], 5, (0, 0, -1))
 
     load_st.wait()
     load_cnt.wait()
 
-    def turn(o, carry):
-        for s in range(4):
-            n = o * 4 + s
-            _, b0, c = place(o, s)
+    def gather(pair, carry):
+        kept = []
+        for u in range(2):
+            n = pair * 2 + u
+            a, b0, c = place(n >> 2, n & 3)
             by = (c + 16 * b0) & 127
             planes = [
                 pltpu.roll(pv[pl.ds(n * 128 + yh * 4 + i, 16, stride=8), :], by, 1)
                 for i in range(4) for yh in range(2)
             ]
+            corner = (16 + b0) * 48 + 16 + a
+            keep = []
+            for y in range(8):
+                z = (lane - 16 * (y + b0)) & 127
+                keep.append((z >= c) & (z < c + 16))
+            acc = [None] * 8
+            for yh in range(2):
+                for h in range(2):
+                    g = []
+                    for b in range(2):
+                        v = jnp.zeros((8, 128), F32)
+                        for y in range(8):
+                            at = b * 2304 + (8 * yh + y) * 48 + 8 * h
+                            v = jnp.where(keep[y], xt[pl.ds(corner + at, 8), :], v)
+                        g.append(v)
+                    for i in range(4):
+                        p = planes[i * 2 + yh][8 * h : 8 * h + 8]
+                        for b in range(2):
+                            term = g[b] * p
+                            k = b * 4 + i
+                            acc[k] = term if acc[k] is None else acc[k] + term
+            kept.append((n, planes, acc))
+        for n, planes, acc in kept:
             for k, plane in enumerate(planes):
                 pr[pl.ds(n * 128 + k * 16, 16), :] = plane
+            for k in range(8):
+                accs[pl.ds(n * 64 + k * 8, 8), :] = acc[k]
         return carry
 
     for k in range(4):
         load_p[k].wait()
-        lax.fori_loop(2 * k, 2 * k + 2, turn, 0)
-
-    def gather(n, carry):
-        o, s = n >> 2, n & 3
-        a, b0, c = place(o, s)
-        corner = (16 + b0) * 48 + 16 + a
-        keep = []
-        for y in range(8):
-            z = (lane - 16 * (y + b0)) & 127
-            keep.append((z >= c) & (z < c + 16))
-        acc = [jnp.zeros((8, 128), F32) for _ in range(8)]
-        for yh in range(2):
-            for h in range(2):
-                g = []
-                for b in range(2):
-                    v = jnp.zeros((8, 128), F32)
-                    for y in range(8):
-                        w = xt[pl.ds(corner + (b * 2304 + (8 * yh + y) * 48 + 8 * h), 8), :]
-                        v = jnp.where(keep[y], w, v)
-                    g.append(v)
-                for i in range(4):
-                    p = pr[pl.ds(n * 128 + i * 32 + yh * 16 + h * 8, 8), :]
-                    for b in range(2):
-                        acc[b * 4 + i] = acc[b * 4 + i] + g[b] * p
-        for k in range(8):
-            accs[pl.ds(n * 64 + k * 8, 8), :] = acc[k]
-        return carry
-
-    lax.fori_loop(0, 32, gather, 0)
+        lax.fori_loop(4 * k, 4 * k + 4, gather, 0)
 
     total = accs[pl.ds(0, 256, stride=8), :]
     for k in range(1, 8):
         total = total + accs[pl.ds(k, 256, stride=8), :]
-    mine = lax.dot_general(jnp.ones((8, 128), F32), total, (((1,), (1,)), ((), ())),
-                           precision=HI, preferred_element_type=F32)
+    mine = exact_dot(total, jnp.ones((8, 128), F32), ((1,), (1,)), flip=True)
     recv[0] = mine[0:1]
     parts = []
     for k, e in enumerate(others):
@@ -202,17 +223,11 @@
         copy.start()
         parts.append(copy)
 
-    row, col = iota((16, 128), 0), iota((16, 128), 1)
-    sel = (col == jnp.where(row < 8, 120 + row, row - 8)).astype(F32)
-    zs[...] = lax.dot_general(sel, fold[...], (((1,), (1,)), ((), ())), precision=HI,
-                              preferred_element_type=F32)
-    send(zs.at[0:8], zr.at[0:8], 4, (0, 0, 1))
-    send(zs.at[8:16], zr.at[8:16], 5, (0, 0, -1))
     load_y.wait()
     load_pot.wait()
     r128, c128 = iota((128, 128), 0), iota((128, 128), 1)
     near = jnp.where(r128 == c128, -0.5 * 3.0 * COEFF[0], band(r128 - c128))
-    out_ref[...] = lax.dot_general(fold[...], near, (((1,), (0,)), ((), ())), precision=HI,
+    base[...] = lax.dot_general(fold[...], near, (((1,), (0,)), ((), ())), precision=HI,
                            preferred_element_type=F32)
     for copy in sends[:4]:
         copy.wait()
@@ -221,7 +236,7 @@
         done = []
         for b in range(2):
             here = pl.ds(b * 256 + x * 16, 16)
-            acc = pot[x] * xe[b, x + 6] + out_ref[here, :]
+            acc = pot[x] * xe[b, x + 6] + base[here, :]
             for k in range(1, 7):
                 four = (ye[b, x, 8 - k : 24 - k, :] + ye[b, x, 8 + k : 24 + k, :]) + (
                     xe[b, x + 6 - k] + xe[b, x + 6 + k]
@@ -229,7 +244,7 @@
                 acc = acc + (-0.5 * COEFF[k]) * four
             done.append(acc)
         for b in range(2):
-            out_ref[pl.ds(b * 256 + x * 16, 16), :] = done[b]
+            base[pl.ds(b * 256 + x * 16, 16), :] = done[b]
         return carry
 
     lax.fori_loop(0, 16, stencil, 0)
@@ -249,14 +264,18 @@
     wide = lax.dot_general(per_row, spread, (((1,), (0,)), ((), ())), precision=HI,
                            preferred_element_type=F32)
     same = iota((256, 256), 0) // 4 == iota((256, 256), 1) // 4
-    mprime[...] = jnp.where(same, wide, 0.0)
+    atom = iota((256, 256), 0) // 8
+    count = jnp.zeros((256, 256), jnp.int32)
+    for o in range(8):
+        count = jnp.where(atom // 4 == o, cnt_ref[o], count)
+    mprime[...] = jnp.where(same & (atom % 4 < count), wide, 0.0)
 
     for copy in sends[4:]:
         copy.wait()
     far = band(jnp.where(row < 8, row - 8, 120 + row) - col)
     edge = lax.dot_general(zr[...], far, (((0,), (0,)), ((), ())), precision=HI,
                            preferred_element_type=F32)
-    out_ref[...] += edge
+    base[...] += edge
 
 
     for copy in parts:
@@ -281,20 +300,17 @@
         up = pltpu.roll(by_z[-1], 32, 1)
         halves.append(by_z[0] + jnp.where(upper_z, up, down))
     sums = jnp.concatenate(halves, axis=1)
-    wrep[...] = lax.dot_general(mprime[...] * sums, jnp.ones((256, 128), F32),
-                                (((1,), (0,)), ((), ())), precision=HI,
-                                preferred_element_type=F32)
+    wrep[...] = exact_dot(mprime[...] * sums, jnp.ones((256, 128), F32), ((1,), (0,)))
 
     def scatter(o, carry):
         spots, mixes = [], []
         for s in range(4):
             n = o * 4 + s
-            live = jnp.where(s < cnt_ref[o], 1.0, 0.0).astype(F32)
             for b in range(2):
                 mix = jnp.zeros((32, 128), F32)
                 for i in range(4):
                     plane = pr[pl.ds(n * 128 + i * 32, 32), :]
-                    mix = mix + plane * (wrep[pl.ds(n * 8 + b * 4 + i, 1), :] * live)
+                    mix = mix + plane * wrep[pl.ds(n * 8 + b * 4 + i, 1), :]
                 mixes.append(mix)
             spots.append(place(o, s))
         for k, mix in enumerate(mixes):
@@ -324,15 +340,21 @@
 
     lax.fori_loop(0, 8, scatter, 0)
 
+    outs = []
     for b in range(2):
         planes = [sheared[b, y] for y in range(16)]
         planes = [
             (pltpu.roll(v, 128 - 16 * (y % 8), 1) if y % 8 else v)
-            + out_ref[pl.ds(b * 256 + y, 16, stride=16), :]
+            + base[pl.ds(b * 256 + y, 16, stride=16), :]
             for y, v in enumerate(planes)
         ]
         for y, v in enumerate(planes):
-            out_ref[pl.ds(b * 256 + y, 16, stride=16), :] = v
+            base[pl.ds(b * 256 + y, 16, stride=16), :] = v
+        half = pl.ds(b * 256, 256)
+        outs.append(pltpu.make_async_copy(base.at[half], out_hbm.at[half], lsem.at[11 + b]))
+        outs[b].start()
+    for copy in outs:
+        copy.wait()
 
 
 def solution(mesh):
@@ -347,13 +369,13 @@
         starts = block_starts.reshape(8, 4, 3).transpose(2, 1, 0)
         counts = owner_counts.reshape(8)
         hbm = pl.BlockSpec(memory_space=pltpu.HBM)
-        vmem = pl.BlockSpec(memory_space=pltpu.VMEM)
         return pl.pallas_call(
             functools.partial(kernel, sizes),
             out_shape=jax.ShapeDtypeStruct((512, 128), F32),
             in_specs=[hbm] * 6,
-            out_specs=vmem,
+            out_specs=hbm,
             scratch_shapes=[
+                pltpu.VMEM((512, 128), F32),
                 pltpu.VMEM((4608, 128), F32),
                 pltpu.VMEM((2, 28, 16, 128), F32),
                 pltpu.VMEM((2, 16, 32, 128), F32),
@@ -373,7 +395,7 @@
                 pltpu.VMEM((4, 4, 4, 8), F32),
                 pltpu.SMEM((3, 4, 8), jnp.int32),
                 pltpu.SMEM((8,), jnp.int32),
-                pltpu.SemaphoreType.DMA((11,)),
+                pltpu.SemaphoreType.DMA((13,)),
                 pltpu.SemaphoreType.DMA((6,)),
                 pltpu.SemaphoreType.DMA((6,)),
                 pltpu.SemaphoreType.DMA((nslots,)),

time: 21.6 us -> 21.4 us (level)
  no operation moved by 1% of the time
where the time goes in v4:
time: 21.4 us; the launch traced here: 21.3 us
  Pallas kernels  19.6 us (92%)
  local copies, waits for them, and re-layouts  1.67 us (8%)
    pallas_call x1, Pallas kernels, on_device(): pl.pallas_call(functools.partial(kernel, sizes), out_shape=jax.ShapeDtype...  19.6 us
    unnamed x1, local copies, waits for them, and re-layouts  1.67 us

profile of v4, /device:TPU:0, one launch (start us, length us, event | category | flops | bytes accessed | tf_op | source)
XLA Modules:
  0.0 21.3 jit_solution(11859879448630024149)
XLA Ops:
  0.0 19.6 %shard_map.64 = f32[512,128]{1,0:T(8,128)} custom-call(f32[2,16,16,128]{3,2,1,0:T(8,128)} %x_hbm.1, f32[16,16,128]{2,1,0:T(8,128)} %pot_hbm.1, f32[4096,128]{1,0:T(8,128)} %bitcast.13, f32[4,4,4,8]{3,2,1,0:T(4,128)} %bitcast.15, s32[3,4,8]{2,1,0:T(4,128)} %bitcast.16, s32[8]{0:T(128)} %bitcast.17), custom_call_target="tpu_custom_call" | custom-call | tf_op jit(solution)/shard_map/pallas_call | solution.py:372
  19.6 1.7 %copy.9 = f32[2,16,16,128]{3,2,1,0:T(8,128)} copy(f32[2,16,16,128]{3,2,1,0:T(8,128)} %bitcast.14) | data formatting | bytes 524288

commit v5 on v4

--- a/solution.py
+++ b/solution.py
@@ -72,8 +72,14 @@
             for ez in res[2]:
                 slots[(ex, ey, ez)] = len(slots)
 
+    near_by = []
+    for d in range(3):
+        up = jnp.where(me[d] == sizes[d] - 1, 0, me[d] + 1)
+        down = jnp.where(me[d] == 0, sizes[d] - 1, me[d] - 1)
+        near_by.append({0: me[d], sizes[d] - 1: down, 1: up})
+
     def device(offset):
-        return tuple(lax.rem(me[d] + offset[d] % sizes[d], sizes[d]) for d in range(3))
+        return tuple(near_by[d][offset[d] % sizes[d]] for d in range(3))
 
     def slot_of(offset):
         return slots[tuple(offset[d] % sizes[d] for d in range(3))]
@@ -81,9 +87,9 @@
     load_x = pltpu.make_async_copy(x_hbm, xe.at[:, 6:22], lsem.at[0])
     load_y = pltpu.make_async_copy(x_hbm, ye.at[:, :, 8:24], lsem.at[1])
     load_p = [
-        pltpu.make_async_copy(p_hbm.at[pl.ds(k * 1024, 1024)], pv.at[pl.ds(k * 1024, 1024)],
+        pltpu.make_async_copy(p_hbm.at[pl.ds(k * 2048, 2048)], pv.at[pl.ds(k * 2048, 2048)],
                               lsem.at[7 + k])
-        for k in range(4)
+        for k in range(2)
     ]
     load_pot = pltpu.make_async_copy(pot_hbm, pot, lsem.at[3])
     load_st = pltpu.make_async_copy(st_hbm, st_ref, lsem.at[4])
@@ -105,7 +111,8 @@
         pl.semaphore_signal(barrier, inc=1, device_id=device(e), device_id_type=MESH)
 
     def clear(i, carry):
-        xt[pl.ds(i * 96, 96), :] = jnp.zeros((96, 128), F32)
+        for b in range(2):
+            xt[b, i] = jnp.zeros((48, 128), F32)
         return carry
 
     lax.fori_loop(0, 48, clear, 0)
@@ -138,7 +145,7 @@
         planes = [fold[pl.ds(b * 256 + y, 16, stride=16), :] for y in range(16)]
         planes = [pltpu.roll(v, 16 * (y % 8), 1) if y % 8 else v for y, v in enumerate(planes)]
         for y, v in enumerate(planes):
-            xt[b * 2304 + (16 + y) * 48 + 16 : b * 2304 + (16 + y) * 48 + 32, :] = v
+            xt[b, 16 + y, 16:32, :] = v
 
     row, col = iota((16, 128), 0), iota((16, 128), 1)
     sel = (col == jnp.where(row < 8, 120 + row, row - 8)).astype(F32)
@@ -165,48 +172,36 @@
     load_st.wait()
     load_cnt.wait()
 
-    def gather(pair, carry):
-        kept = []
-        for u in range(2):
-            n = pair * 2 + u
-            a, b0, c = place(n >> 2, n & 3)
-            by = (c + 16 * b0) & 127
-            planes = [
-                pltpu.roll(pv[pl.ds(n * 128 + yh * 4 + i, 16, stride=8), :], by, 1)
-                for i in range(4) for yh in range(2)
-            ]
-            corner = (16 + b0) * 48 + 16 + a
-            keep = []
-            for y in range(8):
-                z = (lane - 16 * (y + b0)) & 127
-                keep.append((z >= c) & (z < c + 16))
-            acc = [None] * 8
+    def gather(n, carry):
+        a, b0, c = place(n >> 2, n & 3)
+        slabs = [
+            xt[b, pl.ds(16 + b0, 16), pl.ds(16 + a, 16), :] for b in range(2)
+        ]
+        first = lane - 16 * b0
+        parts = [(b, yh, h) for b in range(2) for yh in range(2) for h in range(2)]
+        packed = {k: jnp.zeros((8, 128), F32) for k in parts}
+        for y in range(8):
+            z = (first - 16 * y) & 127
+            keep = (z >= c) & (z < c + 16)
+            for b, yh, h in parts:
+                w = slabs[b][8 * yh + y, 8 * h : 8 * h + 8]
+                packed[b, yh, h] = jnp.where(keep, w, packed[b, yh, h])
+        by = (c + 16 * b0) & 127
+        for i in range(4):
+            acc = [None, None]
             for yh in range(2):
-                for h in range(2):
-                    g = []
-                    for b in range(2):
-                        v = jnp.zeros((8, 128), F32)
-                        for y in range(8):
-                            at = b * 2304 + (8 * yh + y) * 48 + 8 * h
-                            v = jnp.where(keep[y], xt[pl.ds(corner + at, 8), :], v)
-                        g.append(v)
-                    for i in range(4):
-                        p = planes[i * 2 + yh][8 * h : 8 * h + 8]
-                        for b in range(2):
-                            term = g[b] * p
-                            k = b * 4 + i
-                            acc[k] = term if acc[k] is None else acc[k] + term
-            kept.append((n, planes, acc))
-        for n, planes, acc in kept:
-            for k, plane in enumerate(planes):
-                pr[pl.ds(n * 128 + k * 16, 16), :] = plane
-            for k in range(8):
-                accs[pl.ds(n * 64 + k * 8, 8), :] = acc[k]
-        return carry
-
-    for k in range(4):
+                plane = pltpu.roll(pv[pl.ds(n * 128 + yh * 4 + i, 16, stride=8), :], by, 1)
+                pr[pl.ds(n * 128 + i * 32 + yh * 16, 16), :] = plane
+                for b in range(2):
+                    term = (packed[b, yh, 0] * plane[0:8]) + (packed[b, yh, 1] * plane[8:16])
+                    acc[b] = term if acc[b] is None else acc[b] + term
+            for b in range(2):
+                accs[pl.ds(n * 64 + (b * 4 + i) * 8, 8), :] = acc[b]
+        return carry
+
+    for k in range(2):
         load_p[k].wait()
-        lax.fori_loop(4 * k, 4 * k + 4, gather, 0)
+        lax.fori_loop(16 * k, 16 * k + 16, gather, 0)
 
     total = accs[pl.ds(0, 256, stride=8), :]
     for k in range(1, 8):
@@ -254,21 +249,18 @@
     for s in range(4):
         for i in range(4):
             cs[pl.ds((s * 4 + i) * 4, 4), :] = cpl_ref[s, i]
-    pick = (iota((256, 8), 0) // 32 == iota((256, 8), 1)).astype(F32)
-    per_row = lax.dot_general(pick, cs[...], (((1,), (1,)), ((), ())), precision=HI,
-                              preferred_element_type=F32)
-    r64, c64 = iota((256, 64), 0), iota((256, 64), 1)
-    own = ((r64 // 8) % 4 == c64 // 16) & (r64 % 4 == (c64 // 4) % 4)
-    per_row = jnp.where(own, per_row, 0.0)
-    spread = (iota((64, 256), 0) % 4 == iota((64, 256), 1) % 4).astype(F32)
-    wide = lax.dot_general(per_row, spread, (((1,), (0,)), ((), ())), precision=HI,
-                           preferred_element_type=F32)
-    same = iota((256, 256), 0) // 4 == iota((256, 256), 1) // 4
-    atom = iota((256, 256), 0) // 8
-    count = jnp.zeros((256, 256), jnp.int32)
+    pick = (iota((8, 256), 0) == iota((8, 256), 1) // 32).astype(F32)
+    spread = exact_dot(cs[...], pick, ((1,), (0,)))
+    r64, c64 = iota((64, 256), 0), iota((64, 256), 1)
+    own = (r64 // 16 == (c64 // 8) % 4) & (r64 % 4 == c64 % 4)
+    spread = jnp.where(own, spread, 0.0)
+    rows_of = (iota((8, 64), 0) % 4 == (iota((8, 64), 1) // 4) % 4).astype(F32)
+    by_lane = exact_dot(spread, rows_of, ((1,), (0,)), flip=True)
+    lane8 = iota((8, 256), 1)
+    count = jnp.zeros((8, 256), jnp.int32)
     for o in range(8):
-        count = jnp.where(atom // 4 == o, cnt_ref[o], count)
-    mprime[...] = jnp.where(same & (atom % 4 < count), wide, 0.0)
+        count = jnp.where(lane8 // 32 == o, cnt_ref[o], count)
+    mprime[...] = jnp.where((lane8 // 8) % 4 < count, by_lane, 0.0)
 
     for copy in sends[4:]:
         copy.wait()
@@ -299,23 +291,29 @@
         down = pltpu.roll(by_z[1], 96, 1)
         up = pltpu.roll(by_z[-1], 32, 1)
         halves.append(by_z[0] + jnp.where(upper_z, up, down))
-    sums = jnp.concatenate(halves, axis=1)
-    wrep[...] = exact_dot(mprime[...] * sums, jnp.ones((256, 128), F32), ((1,), (0,)))
+    for h in range(2):
+        v = mprime[:, 128 * h : 128 * h + 128] * halves[h]
+        v = v + pltpu.roll(v, 127, 1)
+        v = v + pltpu.roll(v, 126, 1)
+        for g in range(32):
+            wrep[(h * 32 + g) * 8 : (h * 32 + g) * 8 + 8, :] = jnp.broadcast_to(
+                v[:, 4 * g : 4 * g + 1], (8, 128)
+            )
 
     def scatter(o, carry):
-        spots, mixes = [], []
+        spots = []
         for s in range(4):
             n = o * 4 + s
+            planes = pr[pl.ds(n * 128, 128), :]
             for b in range(2):
-                mix = jnp.zeros((32, 128), F32)
+                mix = None
                 for i in range(4):
-                    plane = pr[pl.ds(n * 128 + i * 32, 32), :]
-                    mix = mix + plane * wrep[pl.ds(n * 8 + b * 4 + i, 1), :]
-                mixes.append(mix)
+                    term = planes[i * 32 : i * 32 + 32] * wrep[pl.ds(n * 16 + b * 8 + i, 1), :]
+                    mix = term if mix is None else mix + term
+                for yh in range(2):
+                    at = (s * 12 + b * 6 + 2 + yh) * 48 + 16
+                    zc[at : at + 16, :] = mix[yh * 16 : yh * 16 + 16]
             spots.append(place(o, s))
-        for k, mix in enumerate(mixes):
-            for yh in range(2):
-                zc[(k * 6 + 2 + yh) * 48 + 16 : (k * 6 + 2 + yh) * 48 + 32, :] = mix[yh * 16 : yh * 16 + 16]
         for r in range(8):
             keep = []
             z = (lane - 16 * r) & 127
@@ -376,7 +374,7 @@
             out_specs=hbm,
             scratch_shapes=[
                 pltpu.VMEM((512, 128), F32),
-                pltpu.VMEM((4608, 128), F32),
+                pltpu.VMEM((2, 48, 48, 128), F32),
                 pltpu.VMEM((2, 28, 16, 128), F32),
                 pltpu.VMEM((2, 16, 32, 128), F32),
                 pltpu.VMEM((16, 16, 128), F32),
@@ -388,9 +386,9 @@
                 pltpu.VMEM((16, 512), F32),
                 pltpu.VMEM((nslots, 1, 256), F32),
                 pltpu.VMEM((2304, 128), F32),
-                pltpu.VMEM((256, 128), F32),
+                pltpu.VMEM((512, 128), F32),
                 pltpu.VMEM((64, 8), F32),
-                pltpu.VMEM((256, 256), F32),
+                pltpu.VMEM((8, 256), F32),
                 pltpu.VMEM((512, 128), F32),
                 pltpu.VMEM((4, 4, 4, 8), F32),
                 pltpu.SMEM((3, 4, 8), jnp.int32),

time: 21.4 us -> 20.8 us (0.972)
  Pallas kernels: 19.6 us -> 18.9 us
    pallas_call x1, Pallas kernels: 19.6 us -> 18.9 us  [on_device(): pl.pallas_call(functools.partial(kernel, sizes), out_shape=jax.ShapeDtype...]
where the time goes in v5:
time: 20.8 us; the launch traced here: 20.6 us
  Pallas kernels  18.9 us (91%)
  local copies, waits for them, and re-layouts  1.67 us (8%)
    pallas_call x1, Pallas kernels, on_device(): pl.pallas_call(functools.partial(kernel, sizes), out_shape=jax.ShapeDtype...  18.9 us
    unnamed x1, local copies, waits for them, and re-layouts  1.67 us

profile of v5, /device:TPU:0, one launch (start us, length us, event | category | flops | bytes accessed | tf_op | source)
XLA Modules:
  0.0 20.6 jit_solution(1634697471428317374)
XLA Ops:
  0.0 18.9 %shard_map.64 = f32[512,128]{1,0:T(8,128)} custom-call(f32[2,16,16,128]{3,2,1,0:T(8,128)} %x_hbm.1, f32[16,16,128]{2,1,0:T(8,128)} %pot_hbm.1, f32[4096,128]{1,0:T(8,128)} %bitcast.13, f32[4,4,4,8]{3,2,1,0:T(4,128)} %bitcast.15, s32[3,4,8]{2,1,0:T(4,128)} %bitcast.16, s32[8]{0:T(128)} %bitcast.17), custom_call_target="tpu_custom_call" | custom-call | tf_op jit(solution)/shard_map/pallas_call | solution.py:370
  18.9 1.7 %copy.9 = f32[2,16,16,128]{3,2,1,0:T(8,128)} copy(f32[2,16,16,128]{3,2,1,0:T(8,128)} %bitcast.14) | data formatting | bytes 524288

commit v6 on v5

--- a/solution.py
+++ b/solution.py
@@ -110,46 +110,6 @@
     for e in others:
         pl.semaphore_signal(barrier, inc=1, device_id=device(e), device_id_type=MESH)
 
-    def clear(i, carry):
-        for b in range(2):
-            xt[b, i] = jnp.zeros((48, 128), F32)
-        return carry
-
-    lax.fori_loop(0, 48, clear, 0)
-
-    def clear_mix(i, carry):
-        zc[pl.ds(i * 96, 96), :] = jnp.zeros((96, 128), F32)
-        return carry
-
-    lax.fori_loop(0, 24, clear_mix, 0)
-
-    def clear_sum(i, carry):
-        for b in range(2):
-            sheared[b, i] = jnp.zeros((16, 128), F32)
-        return carry
-
-    lax.fori_loop(0, 16, clear_sum, 0)
-
-    lane = iota((8, 128), 1)
-
-    def place(o, s):
-        a = st_ref[0, s, o] - 16 * (o >> 2)
-        b0 = st_ref[1, s, o] - 16 * ((o >> 1) & 1)
-        c = st_ref[2, s, o] - 128 * (o & 1)
-        return a, b0, c
-
-    load_x.wait()
-
-    fold[...] = xe[:, 6:22].reshape(512, 128)
-    for b in range(2):
-        planes = [fold[pl.ds(b * 256 + y, 16, stride=16), :] for y in range(16)]
-        planes = [pltpu.roll(v, 16 * (y % 8), 1) if y % 8 else v for y, v in enumerate(planes)]
-        for y, v in enumerate(planes):
-            xt[b, 16 + y, 16:32, :] = v
-
-    row, col = iota((16, 128), 0), iota((16, 128), 1)
-    sel = (col == jnp.where(row < 8, 120 + row, row - 8)).astype(F32)
-    zs[...] = exact_dot(fold[...], sel, ((1,), (1,)), flip=True)
     pl.semaphore_wait(barrier, len(others))
 
     sends = []
@@ -166,6 +126,46 @@
     send(x_hbm.at[:, :, 0:8, :], ye.at[:, :, 24:32, :], 1, (0, -1, 0))
     send(x_hbm.at[:, 10:16], xe.at[:, 0:6], 2, (1, 0, 0))
     send(x_hbm.at[:, 0:6], xe.at[:, 22:28], 3, (-1, 0, 0))
+    def clear(i, carry):
+        for b in range(2):
+            xt[b, i] = jnp.zeros((48, 128), F32)
+        return carry
+
+    lax.fori_loop(0, 48, clear, 0)
+
+    def clear_mix(i, carry):
+        zc[pl.ds(i * 96, 96), :] = jnp.zeros((96, 128), F32)
+        return carry
+
+    lax.fori_loop(0, 24, clear_mix, 0)
+
+    def clear_sum(i, carry):
+        for b in range(2):
+            sheared[b, i] = jnp.zeros((16, 128), F32)
+        return carry
+
+    lax.fori_loop(0, 16, clear_sum, 0)
+
+    lane = iota((8, 128), 1)
+
+    def place(o, s):
+        a = st_ref[0, s, o] - 16 * (o >> 2)
+        b0 = st_ref[1, s, o] - 16 * ((o >> 1) & 1)
+        c = st_ref[2, s, o] - 128 * (o & 1)
+        return a, b0, c
+
+    load_x.wait()
+
+    fold[...] = xe[:, 6:22].reshape(512, 128)
+    for b in range(2):
+        planes = [fold[pl.ds(b * 256 + y, 16, stride=16), :] for y in range(16)]
+        planes = [pltpu.roll(v, 16 * (y % 8), 1) if y % 8 else v for y, v in enumerate(planes)]
+        for y, v in enumerate(planes):
+            xt[b, 16 + y, 16:32, :] = v
+
+    row, col = iota((16, 128), 0), iota((16, 128), 1)
+    sel = (col == jnp.where(row < 8, 120 + row, row - 8)).astype(F32)
+    zs[...] = exact_dot(fold[...], sel, ((1,), (1,)), flip=True)
     send(zs.at[0:8], zr.at[0:8], 4, (0, 0, 1))
     send(zs.at[8:16], zr.at[8:16], 5, (0, 0, -1))
 

time: 20.8 us -> 20.7 us (level)
  no operation moved by 1% of the time
where the time goes in v6:
time: 20.7 us; the launch traced here: 20.6 us
  Pallas kernels  18.9 us (91%)
  local copies, waits for them, and re-layouts  1.67 us (8%)
    pallas_call x1, Pallas kernels, on_device(): pl.pallas_call(functools.partial(kernel, sizes), out_shape=jax.ShapeDtype...  18.9 us
    unnamed x1, local copies, waits for them, and re-layouts  1.67 us

profile of v6, /device:TPU:0, one launch (start us, length us, event | category | flops | bytes accessed | tf_op | source)
XLA Modules:
  0.0 20.6 jit_solution(17658917197003762188)
XLA Ops:
  0.0 18.9 %shard_map.64 = f32[512,128]{1,0:T(8,128)} custom-call(f32[2,16,16,128]{3,2,1,0:T(8,128)} %x_hbm.1, f32[16,16,128]{2,1,0:T(8,128)} %pot_hbm.1, f32[4096,128]{1,0:T(8,128)} %bitcast.13, f32[4,4,4,8]{3,2,1,0:T(4,128)} %bitcast.15, s32[3,4,8]{2,1,0:T(4,128)} %bitcast.16, s32[8]{0:T(128)} %bitcast.17), custom_call_target="tpu_custom_call" | custom-call | tf_op jit(solution)/shard_map/pallas_call | solution.py:370
  18.9 1.7 %copy.9 = f32[2,16,16,128]{3,2,1,0:T(8,128)} copy(f32[2,16,16,128]{3,2,1,0:T(8,128)} %bitcast.14) | data formatting | bytes 524288

commit v7 on v5

--- a/solution.py
+++ b/solution.py
@@ -201,7 +201,7 @@
 
     for k in range(2):
         load_p[k].wait()
-        lax.fori_loop(16 * k, 16 * k + 16, gather, 0)
+        lax.fori_loop(16 * k, 16 * k + 16, gather, 0, unroll=2)
 
     total = accs[pl.ds(0, 256, stride=8), :]
     for k in range(1, 8):
@@ -225,7 +225,7 @@
     base[...] = lax.dot_general(fold[...], near, (((1,), (0,)), ((), ())), precision=HI,
                            preferred_element_type=F32)
     for copy in sends[:4]:
-        copy.wait()
+        copy.wait_recv()
 
     def stencil(x, carry):
         done = []
@@ -263,7 +263,7 @@
     mprime[...] = jnp.where((lane8 // 8) % 4 < count, by_lane, 0.0)
 
     for copy in sends[4:]:
-        copy.wait()
+        copy.wait_recv()
     far = band(jnp.where(row < 8, row - 8, 120 + row) - col)
     edge = lax.dot_general(zr[...], far, (((0,), (0,)), ((), ())), precision=HI,
                            preferred_element_type=F32)
@@ -271,7 +271,7 @@
 
 
     for copy in parts:
-        copy.wait()
+        copy.wait_recv()
 
     def got(dx, dy, dz):
         r = recv[slot_of((dx, dy, dz))]
@@ -351,6 +351,8 @@
         half = pl.ds(b * 256, 256)
         outs.append(pltpu.make_async_copy(base.at[half], out_hbm.at[half], lsem.at[11 + b]))
         outs[b].start()
+    for copy in sends + parts:
+        copy.wait_send()
     for copy in outs:
         copy.wait()
 

time: 20.8 us -> 20.8 us (level)
  no operation moved by 1% of the time
where the time goes in v7:
time: 20.8 us; the launch traced here: 20.6 us
  Pallas kernels  18.9 us (91%)
  local copies, waits for them, and re-layouts  1.67 us (8%)
    pallas_call x1, Pallas kernels, on_device(): pl.pallas_call(functools.partial(kernel, sizes), out_shape=jax.ShapeDtype...  18.9 us
    unnamed x1, local copies, waits for them, and re-layouts  1.67 us

profile of v7, /device:TPU:0, one launch (start us, length us, event | category | flops | bytes accessed | tf_op | source)
XLA Modules:
  0.0 20.6 jit_solution(12416306318701880275)
XLA Ops:
  0.0 18.9 %shard_map.64 = f32[512,128]{1,0:T(8,128)} custom-call(f32[2,16,16,128]{3,2,1,0:T(8,128)} %x_hbm.1, f32[16,16,128]{2,1,0:T(8,128)} %pot_hbm.1, f32[4096,128]{1,0:T(8,128)} %bitcast.13, f32[4,4,4,8]{3,2,1,0:T(4,128)} %bitcast.15, s32[3,4,8]{2,1,0:T(4,128)} %bitcast.16, s32[8]{0:T(128)} %bitcast.17), custom_call_target="tpu_custom_call" | custom-call | tf_op jit(solution)/shard_map/pallas_call | solution.py:372
  18.9 1.7 %copy.9 = f32[2,16,16,128]{3,2,1,0:T(8,128)} copy(f32[2,16,16,128]{3,2,1,0:T(8,128)} %bitcast.14) | data formatting | bytes 524288
